TPU v7x, 32 devices: a whole 2x2x4 slice. The times are simulated.
32 devices in a mesh: req: 16 (over z, y, x), hist: 2 (over core).
Axes of the slice: x: 2, y: 2, z: 4, core: 2. Of those that a mesh axis runs over, the one named last changes fastest.
Arguments:
- cand_embed: bfloat16 [16, 768, 1024], P('req', 'hist'), may hold values from -6 to 6
- hist_keys: bfloat16 [16, 256, 1024], P('req', 'hist'), may hold values from -6 to 6
- hist_values: bfloat16 [16, 256, 1024], P('req', 'hist'), may hold values from -6 to 6
- in_weight: bfloat16 [1024, 4096], P('req'), may hold values from -0.1875 to 0.1875
- out_weight: bfloat16 [1024, 1024], replicated, may hold values from -0.1875 to 0.1875
- norm_gain: float32 [1024], replicated, may hold values from 0.25 to 1.75
- cand_counts: int32 [16], P('req'), may hold values from 96 to 768, as said below
- hist_lengths: int32 [16], P('req'), may hold values from 128 to 256, as said below
- self_mask: int32 [16, 768, 64], P('req', 'hist'), may hold values 0 or 1
Outputs:
- cand_out: bfloat16 [16, 768, 1024], P('req', 'hist')
Inputs may be any that keep to these rules, and one draw needn't show every extreme that they name: `cand_counts`: in every draw one request has all 768 candidate slots live; the others have between 96 and 256. `hist_lengths`: multiples of 128; in every draw one request has the full 256.
All inputs are finite; a program needn't handle non-finite values. No bound on the sum of `self_mask` on one device may be relied on, other than what follows from the above.
Results may differ from a plain program's by a relative error of at most 0.0027.
Values may be sent and summed in bfloat16 or wider, within the bound.
A program may use at most 128 MiB of HBM per device.

v0:
```python
import jax
import jax.numpy as jnp
from jax import lax
from jax.sharding import PartitionSpec as P

HEADS = 8
SELF_BLOCK = 64


def on_device(
    cand_embed,
    hist_keys,
    hist_values,
    in_weight,
    out_weight,
    norm_gain,
    cand_counts,
    hist_lengths,
    self_mask,
):
    req_count, cand_count, model_width = cand_embed.shape
    head_dim = model_width // HEADS
    scale_factor = head_dim ** (-0.5)
    flat_rows = cand_embed.reshape(req_count * cand_count, model_width)
    pre_act = jnp.dot(
        flat_rows,
        lax.all_gather(in_weight, "req", axis=0, tiled=True),
        preferred_element_type=jnp.float32,
    )
    projected = (
        jax.nn.silu(pre_act).astype(jnp.bfloat16).reshape(req_count, cand_count, 4 * model_width)
    )
    gate_u = projected[:, :, :model_width]
    self_values = projected[:, :, model_width : 2 * model_width]
    queries = projected[:, :, 2 * model_width : 3 * model_width]
    self_keys = projected[:, :, 3 * model_width :]
    query_heads = queries.reshape(req_count, cand_count, HEADS, head_dim)
    divisor = (hist_lengths + SELF_BLOCK).astype(jnp.float32)
    cand_index = lax.axis_index("hist") * cand_count + jnp.arange(cand_count)
    is_live = cand_index[None, :] < cand_counts[:, None]
    key_part = lax.all_gather(hist_keys, "hist", axis=1, tiled=True)
    value_part = lax.all_gather(hist_values, "hist", axis=1, tiled=True)
    span = key_part.shape[1]
    key_heads = key_part.reshape(req_count, span, HEADS, head_dim)
    value_heads = value_part.reshape(req_count, span, HEADS, head_dim)
    scores = (
        jnp.einsum("rchd,rnhd->rhcn", query_heads, key_heads, preferred_element_type=jnp.float32)
        * scale_factor
    )
    visible = (jnp.arange(span)[None, :] < hist_lengths[:, None]).astype(jnp.float32)
    mixing = (
        jax.nn.silu(scores) * visible[:, None, None, :] / divisor[:, None, None, None]
    ).astype(jnp.bfloat16)
    attended = jnp.einsum(
        "rhcn,rnhd->rchd", mixing, value_heads, preferred_element_type=jnp.float32
    )
    blocks = cand_count // SELF_BLOCK
    query_blocks = queries.reshape(req_count, blocks, SELF_BLOCK, HEADS, head_dim)
    key_blocks = self_keys.reshape(req_count, blocks, SELF_BLOCK, HEADS, head_dim)
    value_blocks = self_values.reshape(req_count, blocks, SELF_BLOCK, HEADS, head_dim)
    self_scores = (
        jnp.einsum(
            "rbphd,rbchd->rbhpc", query_blocks, key_blocks, preferred_element_type=jnp.float32
        )
        * scale_factor
    )
    position = jnp.arange(SELF_BLOCK)
    causal = position[None, :] <= position[:, None]
    diagonal = position[None, :] == position[:, None]
    given = self_mask.reshape(req_count, blocks, SELF_BLOCK, SELF_BLOCK) == 1
    key_live = is_live.reshape(req_count, blocks, 1, SELF_BLOCK)
    allowed = (causal[None, None] & (given | diagonal[None, None]) & key_live).astype(jnp.float32)
    self_mix = (
        jax.nn.silu(self_scores) * allowed[:, :, None, :, :] / divisor[:, None, None, None, None]
    ).astype(jnp.bfloat16)
    self_part = jnp.einsum(
        "rbhpc,rbchd->rbphd", self_mix, value_blocks, preferred_element_type=jnp.float32
    )
    attended = (attended + self_part.reshape(req_count, cand_count, HEADS, head_dim)).reshape(
        req_count, cand_count, model_width
    )
    average = jnp.mean(attended, axis=2, keepdims=True)
    variance = jnp.mean((attended - average) ** 2, axis=2, keepdims=True)
    gated = (
        (attended - average) / jnp.sqrt(variance + 1e-05) * norm_gain * gate_u.astype(jnp.float32)
    ).astype(jnp.bfloat16)
    gated_rows = gated.reshape(req_count * cand_count, model_width)
    branch = jnp.dot(gated_rows, out_weight, preferred_element_type=jnp.float32)
    branch = branch.reshape(req_count, cand_count, model_width)
    result = cand_embed.astype(jnp.float32) + is_live.astype(jnp.float32)[:, :, None] * branch
    return result.astype(jnp.bfloat16)


def solution(mesh):
    in_specs = (
        P("req", "hist", None),
        P("req", "hist", None),
        P("req", "hist", None),
        P("req", None),
        P(),
        P(),
        P("req"),
        P("req"),
        P("req", "hist", None),
    )
    out_specs = P("req", "hist", None)
    return jax.shard_map(
        on_device, mesh=mesh, in_specs=in_specs, out_specs=out_specs, check_vma=False
    )
```

profile of v0, /device:TPU:0, one launch (start us, length us, event | category | flops | bytes accessed | tf_op | source)
XLA Modules:
  0.0 166.9 jit_solution(5197467183300313820)
XLA Ops:
  6.5 0.0 copy-start
  6.5 0.0 copy-start.2
  6.5 0.0 all-gather.2.cloned.1.call-start
  6.5 0.7 all-gather.2.cloned.1.call-update
  7.3 0.0 copy-start.3
  8.0 0.1 copy.35
  8.1 0.9 broadcast_compare_fusion
  9.0 0.1 eq.30
  9.2 0.1 and_convert_fusion
  9.3 0.8 copy.36
  10.8 0.0 copy-done.2
  10.8 2.3 %all_gather.11 = bf16[1,256,1024]{2,1,0:T(8,128)(2,1)S(1)} all-gather(bf16[1,128,1024]{2,1,0:T(8,128)(2,1)S(1)} %copy-done.2), channel_id=1, replica_groups=mesh['req'=16,'hist'=2] {'hist'}, dimensions={1}, use_global_device_ids=true | all-gather | bytes 786432 | tf_op jit(solution)/shard_map/all_gather | solution.py:42
  13.1 1.0 copy.32
  14.1 0.0 copy-done.3
  14.1 0.2 copy.29
  14.3 2.2 %all_gather.10 = bf16[1,256,1024]{1,2,0:T(8,128)(2,1)S(1)} all-gather(bf16[1,128,1024]{1,2,0:T(8,128)(2,1)S(1)} %copy.29), channel_id=1, replica_groups=mesh['req'=16,'hist'=2] {'hist'}, dimensions={1}, use_global_device_ids=true | all-gather | bytes 786432 | tf_op jit(solution)/shard_map/all_gather | solution.py:41
  16.5 109.2 %all-gather.2.cloned.1.call-done = bf16[1024,4096]{1,0:T(8,128)(2,1)} async-done(((bf16[64,4096]{1,0:T(8,128)(2,1)}), bf16[1024,4096]{1,0:T(8,128)(2,1)}) %all-gather.2.cloned.1.call-update) | async-done | bytes 8388624 | tf_op jit(solution)/shard_map/all_gather | solution.py:27
  125.7 7.5 %fusion = bf16[1,384,4096]{2,1,0:T(8,128)(2,1)S(1)} fusion(bf16[1024,4096]{1,0:T(8,128)(2,1)} %all-gather.2.cloned.1.call-done, bf16[1,384,1024]{2,1,0:T(8,128)(2,1)} %param.9), kind=kOutput, calls=%fused_computation.2 | convolution fusion | flops 3229089792 | bytes 12320768 | tf_op jit(solution)/shard_map/dot_general | solution.py:25
  133.2 0.0 copy-start.1
  133.2 0.5 slice_bitcast_fusion.2
  133.7 1.1 copy-done.1
  134.8 0.2 copy.43
  135.0 1.1 copy.45
  136.1 1.1 copy.46
  137.2 3.7 %convolution_bitcast_fusion = f32[1,6,64,8,128]{4,2,3,1,0:T(8,128)} fusion(bf16[6,64,8,128]{3,2,1,0:T(8,128)(2,1)} %bitcast.63, bf16[6,64,8,128]{3,2,1,0:T(8,128)(2,1)} %bitcast.62, bf16[6,64,8,128]{3,2,1,0:T(8,128)(2,1)S(1)} %bitcast.60, f32[]{:T(128)} %bitcast.5, f32[6,64,64]{2,1,0:T(8,128)} %copy.36), kind=kOutput, calls=%fused_computation.9 | convolution fusion | flops 102236160 | bytes 4030468 | tf_op jit(solution)/shard_map/rbhpc,rbchd->rbphd/dot_general | solution.py:76
  140.9 3.5 %copy.38 = f32[1,6,64,8,128]{4,3,2,1,0:T(8,128)} copy(f32[1,6,64,8,128]{4,2,3,1,0:T(8,128)} %convolution_bitcast_fusion) | data formatting | bytes 3145728 | tf_op jit(solution)/shard_map/rbhpc,rbchd->rbphd/transpose | solution.py:76
  144.4 3.0 %copy.39 = f32[1,384,8,128]{1,3,2,0:T(8,128)} copy(f32[1,384,8,128]{3,2,1,0:T(8,128)} %bitcast.59) | data formatting | bytes 3145728 | tf_op jit(solution)/shard_map/reshape | solution.py:79
  147.4 4.3 %fusion.23 = (f32[384]{0:T(512)S(1)}, f32[1,384,8,128]{1,3,2,0:T(8,128)}) fusion(f32[1,384,8,128]{1,3,2,0:T(8,128)} %copy.39, bf16[256,8,128]{0,2,1:T(8,128)(2,1)} %bitcast.65, bf16[256,8,128]{0,2,1:T(8,128)(2,1)S(1)} %bitcast.64, f32[]{:T(128)} %bitcast.5, f32[256]{0:T(256)S(1)} %compare_convert_fusion, bf16[384,8,128]{2,1,0:T(8,128)(2,1)S(1)} %bitcast.61), kind=kOutput, calls=%fused_computation.36 | convolution fusion | flops 409730688 | bytes 4983300 | tf_op jit(solution)/shard_map/rhcn,rnhd->rchd/dot_general | solution.py:54
  151.7 1.6 multiply_reduce_fusion
  153.3 0.0 copy-start.4
  153.3 0.0 copy-start.5
  153.3 3.1 %copy.42 = f32[1,384,1024]{2,1,0:T(8,128)} copy(f32[1,384,1024]{1,2,0:T(8,128)} %bitcast.58) | data formatting | bytes 3145728 | tf_op jit(solution)/shard_map/reshape | solution.py:79
  156.5 0.0 copy-done
  156.5 0.0 copy-done.4
  156.5 0.0 copy-done.5
  156.5 3.6 %fusion.1 = bf16[1,384,1024]{2,1,0:T(8,128)(2,1)} fusion(bf16[1,384,1024]{2,1,0:T(8,128)(2,1)S(1)} %copy-done.4, bf16[1024,1024]{1,0:T(8,128)(2,1)S(1)} %copy-done, f32[1,384,1024]{2,1,0:T(8,128)} %copy.42, bf16[1,384,4096]{2,1,0:T(8,128)(2,1)} %copy-done.1, f32[1024]{0:T(1024)S(1)} %copy-done.5, f32[384]{0:T(512)S(1)} %add_sqrt_fusion, ...), kind=kOutput, calls=%fused_computation.5 | convolution fusion | flops 809238528 | bytes 6038016 | tf_op jit(solution)/shard_map/dot_general | solution.py:88
  (6 shorter events, 0.1 us)
Async XLA Ops:
  6.5 149.9 %copy-start = (bf16[1024,1024]{1,0:T(8,128)(2,1)S(1)}, bf16[1024,1024]{1,0:T(8,128)(2,1)}, u32[]{:S(2)}) copy-start(bf16[1024,1024]{1,0:T(8,128)(2,1)} %param.13) | copy-start | bytes 6291460
  6.5 4.3 %copy-start.2 = (bf16[1,128,1024]{2,1,0:T(8,128)(2,1)S(1)}, bf16[1,128,1024]{2,1,0:T(8,128)(2,1)}, u32[]{:S(2)}) copy-start(bf16[1,128,1024]{2,1,0:T(8,128)(2,1)} %param.11) | copy-start | bytes 786436
  6.5 119.2 %all-gather.2.cloned.1.call-start = ((), (), s32[]{:S(2)}) async-start(), calls=%async_computation | async-start | bytes 8912896 | tf_op jit(solution)/shard_map/all_gather | solution.py:27
  7.3 6.9 %copy-start.3 = (bf16[1,128,1024]{2,1,0:T(8,128)(2,1)S(1)}, bf16[1,128,1024]{2,1,0:T(8,128)(2,1)}, u32[]{:S(2)}) copy-start(bf16[1,128,1024]{2,1,0:T(8,128)(2,1)} %param.10) | copy-start | bytes 786436
  133.2 1.7 copy-start.1
  153.3 3.1 %copy-start.4 = (bf16[1,384,1024]{2,1,0:T(8,128)(2,1)S(1)}, bf16[1,384,1024]{2,1,0:T(8,128)(2,1)}, u32[]{:S(2)}) copy-start(bf16[1,384,1024]{2,1,0:T(8,128)(2,1)} %param.9) | copy-start | bytes 2359300
  153.3 3.1 %copy-start.5 = (f32[1024]{0:T(1024)S(1)}, f32[1024]{0:T(1024)}, u32[]{:S(2)}) copy-start(f32[1024]{0:T(1024)} %param.14) | copy-start | bytes 12292
Sparse Core Ops, SparseCore 0:
  10.1 115.5 all-gather.1
where the time goes:
time: 167 us
  waiting for transfers between devices  110 us (66%)
  matrix products  19.1 us (11%)
  local copies, waits for them, and re-layouts  15.9 us (10%)
  between operations  14.9 us (9%)
  blocking collectives  4.44 us (3%)
  other arithmetic  2.74 us (2%)
    all_gather x1, waiting for transfers between devices, on_device(): lax.all_gather(in_weight, 'req', axis=0, tiled=True)  109 us
    dot_general x1, matrix products, on_device(): jnp.dot(flat_rows, lax.all_gather(in_weight, 'req', axis=0, tiled=True),...  7.5 us
    dot_general x1, matrix products, on_device(): jnp.einsum('rhcn,rnhd->rchd', mixing, value_heads, preferred_element_type...  4.29 us
    unnamed x17, local copies, waits for them, and re-layouts  4.17 us
    dot_general x1, matrix products, on_device(): jnp.einsum('rbhpc,rbchd->rbphd', self_mix, value_blocks, preferred_elemen...  3.7 us
    dot_general x1, matrix products, on_device(): branch = jnp.dot(gated_rows, out_weight, preferred_element_type=jnp.float32)  3.6 us
    transpose x1, local copies, waits for them, and re-layouts, on_device(): jnp.einsum('rbhpc,rbchd->rbphd', self_mix, value_blocks, preferred_elemen...  3.47 us
  transfers between devices with their start and end apart: 1, of which 1 were waited for; matrix products, arithmetic and copies ran while one was open for 2% of the time, Pallas kernels for 0%

commit v1 on v0

--- a/solution.py
+++ b/solution.py
@@ -1,10 +1,401 @@
+import functools
+
 import jax
 import jax.numpy as jnp
 from jax import lax
+from jax.experimental import pallas as pl
+from jax.experimental.pallas import tpu as pltpu
 from jax.sharding import PartitionSpec as P
 
 HEADS = 8
 SELF_BLOCK = 64
+MESH = pl.DeviceIdType.MESH
+LINE = 4
+PLANE = 4
+GROUPS = (2, 3, 1, 0)
+
+
+def interleave(events, work, start):
+    slots = max(len(events) - start, 1)
+    done = 0
+    for at, event in enumerate(events):
+        event()
+        if at >= start:
+            upto = (at - start + 1) * len(work) // slots
+            for job in work[done:upto]:
+                job()
+            done = max(done, upto)
+    for job in work[done:]:
+        job()
+
+
+def silu(x):
+    half = x * 0.5
+    return half + half * jnp.tanh(half)
+
+
+def layer_kernel(
+    cand_hbm, hk_hbm, hv_hbm, w_ref, wout_hbm, gain_ref, count_ref, length_ref, mask_ref,
+    out_ref,
+    cand, hist_k, hist_v, wbuf, wout, mask, amask, q, k, v, att, st_mine, st_other,
+    g_mine, g_send, g_recv,
+    send_x, send_y, send_up, send_down, recv, sib_send, sib_recv, local_sem,
+):
+    rows, width = cand_hbm.shape
+    all_rows = 2 * rows
+    depth = w_ref.shape[0]
+    half = width // 2
+    hist_rows = hk_hbm.shape[0]
+    span = 2 * hist_rows
+    heads = HEADS // 2
+    head_dim = width // HEADS
+    scale = head_dim ** (-0.5)
+
+    me = lax.axis_index("req")
+    core = lax.axis_index("hist")
+    other = 1 - core
+    z = me // PLANE
+    plane = me - z * PLANE
+    y = plane // 2
+    x = plane - 2 * y
+    plane_x = 2 * y + (1 - x)
+    plane_y = 2 * (1 - y) + x
+    plane_d = 2 * (1 - y) + (1 - x)
+    to_x = {"req": z * PLANE + plane_x}
+    to_y = {"req": z * PLANE + plane_y}
+    to_up = {"req": me + PLANE}
+    to_down = {"req": me - PLANE}
+    sibling = {"hist": other}
+    has_up = z < LINE - 1
+    has_down = z > 0
+    near = z + 1 - 2 * (z // 3)
+    far = 3 * (1 - z // 2)
+    near_z = (z, near, 6 - z - near - far, far)
+
+    my_cols = pl.ds(pl.multiple_of(core * half, half), half)
+    other_cols = pl.ds(pl.multiple_of(other * half, half), half)
+    my_rows = pl.ds(pl.multiple_of(core * rows, rows), rows)
+    other_rows = pl.ds(pl.multiple_of(other * rows, rows), rows)
+    my_hist = pl.ds(pl.multiple_of(core * hist_rows, hist_rows), hist_rows)
+    locals_ = [
+        pltpu.make_async_copy(cand_hbm, cand.at[my_rows], local_sem.at[0]),
+        pltpu.make_async_copy(hk_hbm.at[:, my_cols], hist_k.at[my_hist], local_sem.at[1]),
+        pltpu.make_async_copy(hv_hbm.at[:, my_cols], hist_v.at[my_hist], local_sem.at[2]),
+        pltpu.make_async_copy(mask_ref, mask.at[my_rows], local_sem.at[3]),
+        pltpu.make_async_copy(wout_hbm, wout, local_sem.at[4]),
+    ]
+    for copy in locals_:
+        copy.start()
+
+    barrier = pltpu.get_barrier_semaphore()
+
+    def greet(target):
+        pl.semaphore_signal(barrier, inc=1, device_id=target, device_id_type=MESH)
+
+    greet(to_x)
+    greet(to_y)
+    greet(sibling)
+    pl.when(has_up)(lambda: greet(to_up))
+    pl.when(has_down)(lambda: greet(to_down))
+    pl.semaphore_wait(barrier, 3 + (1 - z // (LINE - 1)) + (z + LINE - 2) // (LINE - 1))
+
+    def slot(g, chip):
+        return wbuf.at[g, pl.ds(pl.multiple_of(chip * depth, depth), depth)]
+
+    def remote(src, dst, ssem, rsem, target):
+        return pltpu.make_async_remote_copy(
+            src_ref=src, dst_ref=dst, send_sem=ssem, recv_sem=rsem,
+            device_id=target, device_id_type=MESH,
+        )
+
+    def own_piece(g):
+        start = pl.multiple_of(GROUPS[g] * width + core * half, half)
+        return w_ref.at[:, pl.ds(start, half)]
+
+    def send(g, chip, sem, target, src=None):
+        here = slot(g, chip) if src is None else src
+        remote(here, slot(g, chip), sem, recv.at[g, chip], target).start()
+
+    def arrived(g, chip):
+        remote(slot(g, chip), slot(g, chip), recv.at[g, chip], recv.at[g, chip], to_x).wait_recv()
+
+    def own(g):
+        src = own_piece(g)
+        send(g, me, send_x.at[g, z], to_x, src)
+        send(g, me, send_y.at[g, z], to_y, src)
+        pl.when(has_up)(lambda: send(g, me, send_up.at[g, z], to_up, src))
+        pl.when(has_down)(lambda: send(g, me, send_down.at[g, z], to_down, src))
+
+    def from_line(g, offset):
+        at = z + offset
+        chip = me + offset * PLANE
+
+        def body():
+            arrived(g, chip)
+            if offset < 0:
+                pl.when(has_up)(lambda: send(g, chip, send_up.at[g, at], to_up))
+            else:
+                pl.when(has_down)(lambda: send(g, chip, send_down.at[g, at], to_down))
+            send(g, chip, send_x.at[g, at], to_x)
+            send(g, chip, send_y.at[g, at], to_y)
+
+        pl.when((at >= 0) if offset < 0 else (at < LINE))(body)
+
+    def from_sides(g, step):
+        at = near_z[step]
+        even = at % 2 == 0
+        chip_x = at * PLANE + plane_x
+        chip_y = at * PLANE + plane_y
+        arrived(g, chip_x)
+        pl.when(even)(lambda: send(g, chip_x, send_y.at[g, LINE + at], to_y))
+        arrived(g, chip_y)
+        pl.when(jnp.logical_not(even))(
+            lambda: send(g, chip_y, send_x.at[g, LINE + at], to_x)
+        )
+
+    def from_diagonal(g):
+        for at in near_z:
+            arrived(g, at * PLANE + plane_d)
+
+    def forwards(g):
+        part = functools.partial
+        events = [part(from_line, g, -1), part(from_line, g, 1), part(from_sides, g, 0)]
+        events += [part(from_line, g, -2), part(from_line, g, 2)]
+        events += [part(from_sides, g, 1), part(from_sides, g, 2)]
+        events += [part(from_line, g, -3), part(from_line, g, 3)]
+        if g + 1 < len(GROUPS):
+            events += [part(own, g + 1)]
+        events += [part(from_sides, g, 3)]
+        return events
+
+    own(0)
+
+    sib = [
+        remote(cand_hbm, cand.at[my_rows], sib_send.at[0], sib_recv.at[0], sibling),
+        remote(hk_hbm.at[:, other_cols], hist_k.at[my_hist], sib_send.at[1], sib_recv.at[1], sibling),
+        remote(hv_hbm.at[:, other_cols], hist_v.at[my_hist], sib_send.at[2], sib_recv.at[2], sibling),
+        remote(mask_ref, mask.at[my_rows], sib_send.at[3], sib_recv.at[3], sibling),
+    ]
+    for copy in sib:
+        copy.start()
+
+    for g in range(len(GROUPS)):
+        wbuf[g, pl.ds(pl.multiple_of(me * depth, depth), depth), :] = own_piece(g)[...]
+
+    count = count_ref[0]
+    length = length_ref[0]
+    divisor = (length + SELF_BLOCK).astype(jnp.float32)
+
+    def inputs_here():
+        for copy in locals_:
+            copy.wait()
+        for copy in sib:
+            copy.wait_recv()
+
+    tile = 2 * SELF_BLOCK
+    tiles = all_rows // tile
+
+    def make_mask(t):
+        r0 = t * tile
+        row = lax.broadcasted_iota(jnp.int32, (tile, tile), 0)
+        col = lax.broadcasted_iota(jnp.int32, (tile, tile), 1)
+        given = mask[pl.ds(r0, tile), :]
+        given = jnp.concatenate([given, given], axis=1)
+        keep = (
+            (row // SELF_BLOCK == col // SELF_BLOCK)
+            & (col <= row)
+            & ((given == 1) | (row == col))
+            & (r0 + col < count)
+        )
+        amask[pl.ds(r0, tile), :] = jnp.where(keep, 1.0 / divisor, 0.0)
+
+    def masks():
+        for t in range(tiles):
+            make_mask(t)
+
+    cols = half // 2
+
+    def project(g, dst, r, n):
+        acc = jnp.dot(
+            cand[pl.ds(r * rows, rows), :],
+            wbuf[g, :, pl.ds(n * cols, cols)],
+            preferred_element_type=jnp.float32,
+        )
+        dst[pl.ds(r * rows, rows), pl.ds(n * cols, cols)] = silu(acc).astype(jnp.bfloat16)
+
+    def projections(g, dst):
+        return [functools.partial(project, g, dst, r, n) for n in range(2) for r in range(2)]
+
+    nt = (((1,), (1,)), ((), ()))
+
+    def hist_part(t):
+        r0 = t * tile
+        col = lax.broadcasted_iota(jnp.int32, (1, span), 1)
+        weight = jnp.where(col < length, 1.0 / divisor, 0.0)
+        for h in range(heads):
+            hc = slice(h * head_dim, (h + 1) * head_dim)
+            s = lax.dot_general(
+                q[pl.ds(r0, tile), hc], hist_k[:, hc], nt, preferred_element_type=jnp.float32
+            )
+            mix = (silu(s * scale) * weight).astype(jnp.bfloat16)
+            att[pl.ds(r0, tile), hc] = jnp.dot(
+                mix, hist_v[:, hc], preferred_element_type=jnp.float32
+            )
+
+    def self_part(t):
+        r0 = t * tile
+        for h in range(heads):
+            hc = slice(h * head_dim, (h + 1) * head_dim)
+            s = lax.dot_general(
+                q[pl.ds(r0, tile), hc], k[pl.ds(r0, tile), hc], nt,
+                preferred_element_type=jnp.float32,
+            )
+            mix = (silu(s * scale) * amask[pl.ds(r0, tile), :]).astype(jnp.bfloat16)
+            att[pl.ds(r0, tile), hc] += jnp.dot(
+                mix, v[pl.ds(r0, tile), hc], preferred_element_type=jnp.float32
+            )
+        here = att[pl.ds(r0, tile), :]
+        mean = jnp.mean(here, axis=1, keepdims=True)
+        spread = jnp.sum((here - mean) ** 2, axis=1, keepdims=True)
+        lane = lax.broadcasted_iota(jnp.int32, (tile, 128), 1)
+        st_mine[pl.ds(r0, tile), :] = jnp.where(lane < 64, mean, spread)
+
+    stats = remote(st_mine, st_other, sib_send.at[4], sib_recv.at[4], sibling)
+
+    def normalise(t):
+        r0 = t * tile
+        mine, theirs = st_mine[pl.ds(r0, tile), :], st_other[pl.ds(r0, tile), :]
+        mean_a, mean_b = mine[:, 0:1], theirs[:, 0:1]
+        gap = mean_a - mean_b
+        mean = 0.5 * (mean_a + mean_b)
+        variance = (mine[:, 64:65] + theirs[:, 64:65] + gap * gap * (half / 2)) / width
+        factor = lax.rsqrt(variance + 1e-05)
+        att[pl.ds(r0, tile), :] = (
+            (att[pl.ds(r0, tile), :] - mean) * factor * gain_ref[:, my_cols]
+        )
+
+    part = functools.partial
+    interleave(forwards(0), [], 0)
+    inputs_here()
+    masks()
+    interleave(
+        forwards(1)[:4] + [part(from_diagonal, 0)] + forwards(1)[4:], projections(0, q), 4
+    )
+    work = projections(1, k) + [part(hist_part, t) for t in range(tiles)]
+    interleave(forwards(2)[:4] + [part(from_diagonal, 1)] + forwards(2)[4:], work, 4)
+    work = projections(2, v) + [part(self_part, t) for t in range(tiles)]
+    work += [stats.start]
+    interleave(forwards(3)[:4] + [part(from_diagonal, 2)] + forwards(3)[4:], work, 4)
+    stats.wait_recv()
+    for t in range(tiles):
+        normalise(t)
+
+    def gate(dst, at):
+        for n in range(2):
+            nc = pl.ds(n * cols, cols)
+            acc = jnp.dot(
+                cand[at, :], wbuf[3, :, nc], preferred_element_type=jnp.float32
+            )
+            u = silu(acc).astype(jnp.bfloat16).astype(jnp.float32)
+            dst[:, nc] = (att[at, nc] * u).astype(jnp.bfloat16)
+
+    from_diagonal(3)
+    gate(g_send, other_rows)
+    gated = remote(g_send, g_recv, sib_send.at[5], sib_recv.at[5], sibling)
+    gated.start()
+    gate(g_mine, my_rows)
+    live_row = core * rows + lax.broadcasted_iota(jnp.int32, (rows, 1), 0)
+    live = jnp.where(live_row < count, 1.0, 0.0)
+    for n in range(4):
+        nc = slice(n * 256, (n + 1) * 256)
+        att_cols = pl.ds((n % 2) * 256, 256)
+        att[pl.ds((n // 2) * rows, rows), att_cols] = jnp.dot(
+            g_mine[...], wout[my_cols, nc], preferred_element_type=jnp.float32
+        )
+    gated.wait_recv()
+    for n in range(4):
+        nc = slice(n * 256, (n + 1) * 256)
+        att_cols = pl.ds((n % 2) * 256, 256)
+        branch = att[pl.ds((n // 2) * rows, rows), att_cols] + jnp.dot(
+            g_recv[...], wout[other_cols, nc], preferred_element_type=jnp.float32
+        )
+        res = cand[my_rows, nc].astype(jnp.float32) + live * branch
+        out_ref[:, nc] = res.astype(jnp.bfloat16)
+
+    for copy in sib:
+        copy.wait_send()
+    stats.wait_send()
+    gated.wait_send()
+
+    def left(sem):
+        piece = slot(0, 0)
+        remote(piece, piece, sem, sem, to_x).wait_send()
+
+    for g in range(len(GROUPS)):
+        for at in range(LINE):
+            left(send_x.at[g, at])
+            left(send_y.at[g, at])
+            if at % 2 == 0:
+                left(send_y.at[g, LINE + at])
+            else:
+                left(send_x.at[g, LINE + at])
+            pl.when(has_up & (at <= z))(lambda: left(send_up.at[g, at]))
+            pl.when(has_down & (at >= z))(lambda: left(send_down.at[g, at]))
+
+
+def on_device_kernel(
+    cand_embed, hist_keys, hist_values, in_weight, out_weight, norm_gain,
+    cand_counts, hist_lengths, self_mask,
+):
+    _, rows, width = cand_embed.shape
+    hist_rows = hist_keys.shape[1]
+    half = width // 2
+    depth = in_weight.shape[0]
+    bf16, f32 = jnp.bfloat16, jnp.float32
+    groups = len(GROUPS)
+    vmem = pl.BlockSpec(memory_space=pltpu.VMEM)
+    smem = pl.BlockSpec(memory_space=pltpu.SMEM)
+    hbm = pl.BlockSpec(memory_space=pl.ANY)
+    dma = pltpu.SemaphoreType.DMA
+    out = pl.pallas_call(
+        layer_kernel,
+        out_shape=jax.ShapeDtypeStruct((rows, width), bf16),
+        in_specs=[hbm, hbm, hbm, vmem, hbm, vmem, smem, smem, vmem],
+        out_specs=vmem,
+        scratch_shapes=[
+            pltpu.VMEM((2 * rows, width), bf16),
+            pltpu.VMEM((2 * hist_rows, half), bf16),
+            pltpu.VMEM((2 * hist_rows, half), bf16),
+            pltpu.VMEM((groups, width, half), bf16),
+            pltpu.VMEM((width, width), bf16),
+            pltpu.VMEM((2 * rows, SELF_BLOCK), jnp.int32),
+            pltpu.VMEM((2 * rows, 2 * SELF_BLOCK), f32),
+            pltpu.VMEM((2 * rows, half), bf16),
+            pltpu.VMEM((2 * rows, half), bf16),
+            pltpu.VMEM((2 * rows, half), bf16),
+            pltpu.VMEM((2 * rows, half), f32),
+            pltpu.VMEM((2 * rows, 128), f32),
+            pltpu.VMEM((2 * rows, 128), f32),
+            pltpu.VMEM((rows, half), bf16),
+            pltpu.VMEM((rows, half), bf16),
+            pltpu.VMEM((rows, half), bf16),
+            dma((groups, 2 * LINE)),
+            dma((groups, 2 * LINE)),
+            dma((groups, LINE)),
+            dma((groups, LINE)),
+            dma((groups, LINE * PLANE)),
+            dma((6,)),
+            dma((6,)),
+            dma((5,)),
+        ],
+        compiler_params=pltpu.CompilerParams(
+            collective_id=0, has_side_effects=True, vmem_limit_bytes=40 * 1024 * 1024
+        ),
+    )(
+        cand_embed[0], hist_keys[0], hist_values[0], in_weight, out_weight,
+        norm_gain[None, :], cand_counts, hist_lengths, self_mask[0],
+    )
+    return out[None]
 
 
 def on_device(
@@ -104,6 +495,8 @@
         P("req", "hist", None),
     )
     out_specs = P("req", "hist", None)
+    paired = mesh.shape["hist"] == 2 and mesh.shape["req"] == LINE * PLANE
     return jax.shard_map(
-        on_device, mesh=mesh, in_specs=in_specs, out_specs=out_specs, check_vma=False
-    )
+        on_device_kernel if paired else on_device,
+        mesh=mesh, in_specs=in_specs, out_specs=out_specs, check_vma=False,
+    )

time: 167 us -> 74.6 us (0.45)
  waiting for transfers between devices: 110 us -> 0 us
  Pallas kernels: 0 us -> 64.6 us
  matrix products: 19.1 us -> 0 us
  between operations: 14.9 us -> 1.32 us
  local copies, waits for them, and re-layouts: 15.9 us -> 8.25 us
  blocking collectives: 4.44 us -> 0 us
  other arithmetic: 2.74 us -> 0 us
    all_gather x1 -> x0, waiting for transfers between devices: 109 us -> none  [on_device(): lax.all_gather(in_weight, 'req', axis=0, tiled=True)]
    pallas_call x0 -> x1, Pallas kernels: none -> 64.6 us  [on_device_kernel(): pl.pallas_call(layer_kernel, out_shape=jax.ShapeDtypeStruct((rows, width)...]
    dot_general x4 -> x0, matrix products: 19.1 us -> none  [the longest x1 7.5 us: on_device(): jnp.dot(flat_rows, lax.all_gather(in_weight, 'req', axis=0, tiled=True),...]
    reshape x2 -> x0, local copies, waits for them, and re-layouts: 6.13 us -> none  [the longest x1 3.11 us: on_device(): (attended + self_part.reshape(req_count, cand_count, HEADS, head_dim)).re...]
    all_gather x2 -> x0, blocking collectives: 4.44 us -> none  [the longest x1 2.26 us: on_device(): value_part = lax.all_gather(hist_values, 'hist', axis=1, tiled=True)]
    unnamed x17 -> x14, local copies, waits for them, and re-layouts: 4.17 us -> 8.25 us
    transpose x1 -> x0, local copies, waits for them, and re-layouts: 3.47 us -> none  [on_device(): jnp.einsum('rbhpc,rbchd->rbphd', self_mix, value_blocks, preferred_elemen...]
  transfers between devices with their start and end apart: 1 -> 0, of which waited for: 1 -> 0; matrix products, arithmetic and copies ran while one was open for 2% -> 0% of each run, Pallas kernels for 0% -> 0%
where the time goes in v1:
time: 74.6 us; the launch traced here: 74.1 us
  Pallas kernels  64.6 us (87%)
  local copies, waits for them, and re-layouts  8.25 us (11%)
  between operations  1.32 us (2%)
    pallas_call x1, Pallas kernels, on_device_kernel(): pl.pallas_call(layer_kernel, out_shape=jax.ShapeDtypeStruct((rows, width)...  64.6 us
    unnamed x14, local copies, waits for them, and re-layouts  8.25 us

profile of v1, /device:TPU:0, one launch (start us, length us, event | category | flops | bytes accessed | tf_op | source)
XLA Modules:
  0.0 74.1 jit_solution(15463499423103557139)
XLA Ops:
  1.3 1.0 %copy.10 = s32[1,384,64]{2,1,0:T(8,128)S(1)} copy(s32[1,384,64]{1,2,0:T(8,128)} %param.17) | data formatting | bytes 196608 | tf_op args[8]
  2.3 0.0 copy-start
  2.3 1.6 %copy-done = bf16[1024,1024]{1,0:T(8,128)(2,1)S(1)} copy-done((bf16[1024,1024]{1,0:T(8,128)(2,1)S(1)}, bf16[1024,1024]{1,0:T(8,128)(2,1)}, u32[]{:S(2)}) %copy-start) | copy-done | bytes 2097176
  3.9 0.0 copy-start.1
  3.9 1.1 %copy-done.1 = bf16[1,384,1024]{2,1,0:T(8,128)(2,1)S(1)} copy-done((bf16[1,384,1024]{2,1,0:T(8,128)(2,1)S(1)}, bf16[1,384,1024]{2,1,0:T(8,128)(2,1)}, u32[]{:S(2)}) %copy-start.1) | copy-done | bytes 786456
  5.1 0.0 copy-start.2
  5.1 1.0 %copy-done.2 = bf16[64,4096]{1,0:T(8,128)(2,1)S(1)} copy-done((bf16[64,4096]{1,0:T(8,128)(2,1)S(1)}, bf16[64,4096]{1,0:T(8,128)(2,1)}, u32[]{:S(2)}) %copy-start.2) | copy-done | bytes 524312
  6.1 0.0 copy-start.3
  6.1 0.9 %copy-done.3 = bf16[1,128,1024]{2,1,0:T(8,128)(2,1)S(1)} copy-done((bf16[1,128,1024]{2,1,0:T(8,128)(2,1)S(1)}, bf16[1,128,1024]{2,1,0:T(8,128)(2,1)}, u32[]{:S(2)}) %copy-start.3) | copy-done | bytes 262168
  7.0 0.0 copy-start.4
  7.0 0.9 %copy-done.4 = bf16[1,128,1024]{2,1,0:T(8,128)(2,1)S(1)} copy-done((bf16[1,128,1024]{2,1,0:T(8,128)(2,1)S(1)}, bf16[1,128,1024]{2,1,0:T(8,128)(2,1)}, u32[]{:S(2)}) %copy-start.4) | copy-done | bytes 262168
  8.0 0.0 copy-start.5
  8.0 0.7 copy-done.5
  8.7 64.6 %shard_map.91 = bf16[384,1024]{1,0:T(8,128)(2,1)S(1)} custom-call(bf16[384,1024]{1,0:T(8,128)(2,1)S(1)} %bitcast.8, bf16[128,1024]{1,0:T(8,128)(2,1)S(1)} %bitcast.9, bf16[128,1024]{1,0:T(8,128)(2,1)S(1)} %bitcast.10, bf16[64,4096]{1,0:T(8,128)(2,1)S(1)} %copy-done.2, bf16[1024,1024]{1,0:T(8,128)(2,1)S(1)} %copy-done, f32[1,1024]{1,0:T(1,128)S(1)} %bitcast.11, ...), custom_call_target="tpu_custom_call" | custom-call | tf_op jit(solution)/shard_map/pallas_call | solution.py:360
  73.3 0.9 %copy.14 = bf16[1,384,1024]{2,1,0:T(8,128)(2,1)} copy(bf16[1,384,1024]{2,1,0:T(8,128)(2,1)S(1)} %bitcast.6) | data formatting | bytes 1572864
Async XLA Ops:
  2.3 1.6 %copy-start = (bf16[1024,1024]{1,0:T(8,128)(2,1)S(1)}, bf16[1024,1024]{1,0:T(8,128)(2,1)}, u32[]{:S(2)}) copy-start(bf16[1024,1024]{1,0:T(8,128)(2,1)} %wout_hbm.1) | copy-start | bytes 6291460
  3.9 1.1 %copy-start.1 = (bf16[1,384,1024]{2,1,0:T(8,128)(2,1)S(1)}, bf16[1,384,1024]{2,1,0:T(8,128)(2,1)}, u32[]{:S(2)}) copy-start(bf16[1,384,1024]{2,1,0:T(8,128)(2,1)} %param.9) | copy-start | bytes 2359300
  5.1 1.0 %copy-start.2 = (bf16[64,4096]{1,0:T(8,128)(2,1)S(1)}, bf16[64,4096]{1,0:T(8,128)(2,1)}, u32[]{:S(2)}) copy-start(bf16[64,4096]{1,0:T(8,128)(2,1)} %w_ref.1) | copy-start | bytes 1572868
  6.1 0.9 %copy-start.3 = (bf16[1,128,1024]{2,1,0:T(8,128)(2,1)S(1)}, bf16[1,128,1024]{2,1,0:T(8,128)(2,1)}, u32[]{:S(2)}) copy-start(bf16[1,128,1024]{2,1,0:T(8,128)(2,1)} %param.10) | copy-start | bytes 786436
  7.0 0.9 %copy-start.4 = (bf16[1,128,1024]{2,1,0:T(8,128)(2,1)S(1)}, bf16[1,128,1024]{2,1,0:T(8,128)(2,1)}, u32[]{:S(2)}) copy-start(bf16[1,128,1024]{2,1,0:T(8,128)(2,1)} %param.11) | copy-start | bytes 786436
  8.0 0.7 copy-start.5

commit v2 on v1

--- a/solution.py
+++ b/solution.py
@@ -35,9 +35,9 @@
 
 
 def layer_kernel(
-    cand_hbm, hk_hbm, hv_hbm, w_ref, wout_hbm, gain_ref, count_ref, length_ref, mask_ref,
+    cand_hbm, hk_hbm, hv_hbm, w_ref, wout_hbm, gain_hbm, count_ref, length_ref, mask_ref,
     out_ref,
-    cand, hist_k, hist_v, wbuf, wout, mask, amask, q, k, v, att, st_mine, st_other,
+    gain, cand, hist_k, hist_v, wbuf, wout, mask, amask, q, k, v, att, st_mine, st_other,
     g_mine, g_send, g_recv,
     send_x, send_y, send_up, send_down, recv, sib_send, sib_recv, local_sem,
 ):
@@ -81,9 +81,19 @@
         pltpu.make_async_copy(cand_hbm, cand.at[my_rows], local_sem.at[0]),
         pltpu.make_async_copy(hk_hbm.at[:, my_cols], hist_k.at[my_hist], local_sem.at[1]),
         pltpu.make_async_copy(hv_hbm.at[:, my_cols], hist_v.at[my_hist], local_sem.at[2]),
-        pltpu.make_async_copy(mask_ref, mask.at[my_rows], local_sem.at[3]),
+        pltpu.make_async_copy(mask_ref, mask.at[core], local_sem.at[3]),
         pltpu.make_async_copy(wout_hbm, wout, local_sem.at[4]),
+        pltpu.make_async_copy(gain_hbm, gain, local_sem.at[5]),
     ]
+    for g, base in enumerate(GROUPS):
+        start = pl.multiple_of(base * width + core * half, half)
+        locals_.append(
+            pltpu.make_async_copy(
+                w_ref.at[:, pl.ds(start, half)],
+                wbuf.at[g, pl.ds(pl.multiple_of(me * depth, depth), depth)],
+                local_sem.at[6 + g],
+            )
+        )
     for copy in locals_:
         copy.start()
 
@@ -174,13 +184,10 @@
         remote(cand_hbm, cand.at[my_rows], sib_send.at[0], sib_recv.at[0], sibling),
         remote(hk_hbm.at[:, other_cols], hist_k.at[my_hist], sib_send.at[1], sib_recv.at[1], sibling),
         remote(hv_hbm.at[:, other_cols], hist_v.at[my_hist], sib_send.at[2], sib_recv.at[2], sibling),
-        remote(mask_ref, mask.at[my_rows], sib_send.at[3], sib_recv.at[3], sibling),
+        remote(mask_ref, mask.at[core], sib_send.at[3], sib_recv.at[3], sibling),
     ]
     for copy in sib:
         copy.start()
-
-    for g in range(len(GROUPS)):
-        wbuf[g, pl.ds(pl.multiple_of(me * depth, depth), depth), :] = own_piece(g)[...]
 
     count = count_ref[0]
     length = length_ref[0]
@@ -199,8 +206,8 @@
         r0 = t * tile
         row = lax.broadcasted_iota(jnp.int32, (tile, tile), 0)
         col = lax.broadcasted_iota(jnp.int32, (tile, tile), 1)
-        given = mask[pl.ds(r0, tile), :]
-        given = jnp.concatenate([given, given], axis=1)
+        given = mask[r0 // rows, :, pl.ds(r0 % rows, tile)]
+        given = jnp.concatenate([given, given], axis=0).T
         keep = (
             (row // SELF_BLOCK == col // SELF_BLOCK)
             & (col <= row)
@@ -271,7 +278,7 @@
         variance = (mine[:, 64:65] + theirs[:, 64:65] + gap * gap * (half / 2)) / width
         factor = lax.rsqrt(variance + 1e-05)
         att[pl.ds(r0, tile), :] = (
-            (att[pl.ds(r0, tile), :] - mean) * factor * gain_ref[:, my_cols]
+            (att[pl.ds(r0, tile), :] - mean) * factor * gain[:, my_cols]
         )
 
     part = functools.partial
@@ -360,15 +367,16 @@
     out = pl.pallas_call(
         layer_kernel,
         out_shape=jax.ShapeDtypeStruct((rows, width), bf16),
-        in_specs=[hbm, hbm, hbm, vmem, hbm, vmem, smem, smem, vmem],
+        in_specs=[hbm, hbm, hbm, hbm, hbm, hbm, smem, smem, hbm],
         out_specs=vmem,
         scratch_shapes=[
+            pltpu.VMEM((1, width), f32),
             pltpu.VMEM((2 * rows, width), bf16),
             pltpu.VMEM((2 * hist_rows, half), bf16),
             pltpu.VMEM((2 * hist_rows, half), bf16),
             pltpu.VMEM((groups, width, half), bf16),
             pltpu.VMEM((width, width), bf16),
-            pltpu.VMEM((2 * rows, SELF_BLOCK), jnp.int32),
+            pltpu.VMEM((2, SELF_BLOCK, rows), jnp.int32),
             pltpu.VMEM((2 * rows, 2 * SELF_BLOCK), f32),
             pltpu.VMEM((2 * rows, half), bf16),
             pltpu.VMEM((2 * rows, half), bf16),
@@ -386,14 +394,14 @@
             dma((groups, LINE * PLANE)),
             dma((6,)),
             dma((6,)),
-            dma((5,)),
+            dma((6 + groups,)),
         ],
         compiler_params=pltpu.CompilerParams(
-            collective_id=0, has_side_effects=True, vmem_limit_bytes=40 * 1024 * 1024
+            collective_id=0, has_side_effects=True, vmem_limit_bytes=60 * 1024 * 1024
         ),
     )(
         cand_embed[0], hist_keys[0], hist_values[0], in_weight, out_weight,
-        norm_gain[None, :], cand_counts, hist_lengths, self_mask[0],
+        norm_gain[None, :], cand_counts, hist_lengths, self_mask[0].T,
     )
     return out[None]
 

time: 74.6 us -> 70.1 us (0.940)
  local copies, waits for them, and re-layouts: 8.25 us -> 2.06 us
  Pallas kernels: 64.6 us -> 66.6 us
    unnamed x14 -> x1, local copies, waits for them, and re-layouts: 8.25 us -> 2.06 us
    pallas_call x1, Pallas kernels: 64.6 us -> 66.6 us  [on_device_kernel(): pl.pallas_call(layer_kernel, out_shape=jax.ShapeDtypeStruct((rows, width)...]
where the time goes in v2:
time: 70.1 us; the launch traced here: 70 us
  Pallas kernels  66.6 us (95%)
  local copies, waits for them, and re-layouts  2.06 us (3%)
  between operations  1.3 us (2%)
    pallas_call x1, Pallas kernels, on_device_kernel(): pl.pallas_call(layer_kernel, out_shape=jax.ShapeDtypeStruct((rows, width)...  66.6 us
    unnamed x1, local copies, waits for them, and re-layouts  2.06 us

profile of v2, /device:TPU:0, one launch (start us, length us, event | category | flops | bytes accessed | tf_op | source)
XLA Modules:
  0.0 70.0 jit_solution(12874424181685875847)
XLA Ops:
  1.3 66.6 %shard_map.91 = bf16[384,1024]{1,0:T(8,128)(2,1)} custom-call(bf16[384,1024]{1,0:T(8,128)(2,1)} %bitcast.9, bf16[128,1024]{1,0:T(8,128)(2,1)} %bitcast.10, bf16[128,1024]{1,0:T(8,128)(2,1)} %bitcast.11, bf16[64,4096]{1,0:T(8,128)(2,1)} %w_ref.1, bf16[1024,1024]{1,0:T(8,128)(2,1)} %wout_hbm.1, f32[1,1024]{1,0:T(1,128)} %bitcast.13, s32[1]{0:T(128)S(6)} %copy.11.count_ref, ...), custom_call_target="tpu_custom_call" | custom-call | tf_op jit(solution)/shard_map/pallas_call | solution.py:367
  67.9 2.1 %copy.13 = bf16[1,384,1024]{2,1,0:T(8,128)(2,1)} copy(bf16[1,384,1024]{2,1,0:T(8,128)(2,1)} %bitcast.8) | data formatting | bytes 1572864

commit v3 on v2

--- a/solution.py
+++ b/solution.py
@@ -153,29 +153,43 @@
 
     def from_sides(g, step):
         at = near_z[step]
-        even = at % 2 == 0
+        passed_on = (at % (LINE - 1) == 0) | (at == z)
+        even = (at + g) % 2 == 0
         chip_x = at * PLANE + plane_x
         chip_y = at * PLANE + plane_y
         arrived(g, chip_x)
-        pl.when(even)(lambda: send(g, chip_x, send_y.at[g, LINE + at], to_y))
+        pl.when(passed_on & even)(lambda: send(g, chip_x, send_y.at[g, LINE + at], to_y))
         arrived(g, chip_y)
-        pl.when(jnp.logical_not(even))(
+        pl.when(passed_on & jnp.logical_not(even))(
             lambda: send(g, chip_y, send_x.at[g, LINE + at], to_x)
         )
 
+    def from_corner(g, step):
+        at = near_z[step]
+        chip = at * PLANE + plane_d
+        inner = at % (LINE - 1) != 0
+        arrived(g, chip)
+        pl.when(inner & has_up & (z >= at))(
+            lambda: send(g, chip, send_up.at[g, LINE + at], to_up)
+        )
+        pl.when(inner & has_down & (z <= at))(
+            lambda: send(g, chip, send_down.at[g, LINE + at], to_down)
+        )
+
     def from_diagonal(g):
-        for at in near_z:
-            arrived(g, at * PLANE + plane_d)
+        from_corner(g, 2)
+        from_corner(g, 3)
 
     def forwards(g):
         part = functools.partial
         events = [part(from_line, g, -1), part(from_line, g, 1), part(from_sides, g, 0)]
         events += [part(from_line, g, -2), part(from_line, g, 2)]
         events += [part(from_sides, g, 1), part(from_sides, g, 2)]
+        events += [part(from_corner, g, 0)]
         events += [part(from_line, g, -3), part(from_line, g, 3)]
         if g + 1 < len(GROUPS):
             events += [part(own, g + 1)]
-        events += [part(from_sides, g, 3)]
+        events += [part(from_sides, g, 3), part(from_corner, g, 1)]
         return events
 
     own(0)
@@ -342,10 +356,14 @@
         for at in range(LINE):
             left(send_x.at[g, at])
             left(send_y.at[g, at])
-            if at % 2 == 0:
-                left(send_y.at[g, LINE + at])
+            passed_on = at % (LINE - 1) == 0
+            side = send_y if (at + g) % 2 == 0 else send_x
+            if passed_on:
+                left(side.at[g, LINE + at])
             else:
-                left(send_x.at[g, LINE + at])
+                pl.when(z == at)(lambda: left(side.at[g, LINE + at]))
+                pl.when(has_up & (z >= at))(lambda: left(send_up.at[g, LINE + at]))
+                pl.when(has_down & (z <= at))(lambda: left(send_down.at[g, LINE + at]))
             pl.when(has_up & (at <= z))(lambda: left(send_up.at[g, at]))
             pl.when(has_down & (at >= z))(lambda: left(send_down.at[g, at]))
 
@@ -389,8 +407,8 @@
             pltpu.VMEM((rows, half), bf16),
             dma((groups, 2 * LINE)),
             dma((groups, 2 * LINE)),
-            dma((groups, LINE)),
-            dma((groups, LINE)),
+            dma((groups, 2 * LINE)),
+            dma((groups, 2 * LINE)),
             dma((groups, LINE * PLANE)),
             dma((6,)),
             dma((6,)),

time: 70.1 us -> 70.4 us (level)
  no operation moved by 1% of the time
where the time goes in v3:
time: 70.4 us; the launch traced here: 70.2 us
  Pallas kernels  66.9 us (95%)
  local copies, waits for them, and re-layouts  2.06 us (3%)
  between operations  1.3 us (2%)
    pallas_call x1, Pallas kernels, on_device_kernel(): pl.pallas_call(layer_kernel, out_shape=jax.ShapeDtypeStruct((rows, width)...  66.9 us
    unnamed x1, local copies, waits for them, and re-layouts  2.06 us

profile of v3, /device:TPU:0, one launch (start us, length us, event | category | flops | bytes accessed | tf_op | source)
XLA Modules:
  0.0 70.2 jit_solution(5608720376387910890)
XLA Ops:
  1.3 66.9 %shard_map.91 = bf16[384,1024]{1,0:T(8,128)(2,1)} custom-call(bf16[384,1024]{1,0:T(8,128)(2,1)} %bitcast.9, bf16[128,1024]{1,0:T(8,128)(2,1)} %bitcast.10, bf16[128,1024]{1,0:T(8,128)(2,1)} %bitcast.11, bf16[64,4096]{1,0:T(8,128)(2,1)} %w_ref.1, bf16[1024,1024]{1,0:T(8,128)(2,1)} %wout_hbm.1, f32[1,1024]{1,0:T(1,128)} %bitcast.13, s32[1]{0:T(128)S(6)} %copy.11.count_ref, ...), custom_call_target="tpu_custom_call" | custom-call | tf_op jit(solution)/shard_map/pallas_call | solution.py:385
  68.2 2.1 %copy.13 = bf16[1,384,1024]{2,1,0:T(8,128)(2,1)} copy(bf16[1,384,1024]{2,1,0:T(8,128)(2,1)} %bitcast.8) | data formatting | bytes 1572864
